TPU v7x, 32 devices: a whole 2x2x4 slice. The times are simulated.
32 devices in a mesh: gx: 4 (over y, x), gy: 8 (over z, core).
Axes of the slice: x: 2, y: 2, z: 4, core: 2. Of those that a mesh axis runs over, the one named last changes fastest.
Arguments:
- samples: float32 [2048, 512], replicated, may hold values from -1 to 1
- real_idx: int32 [8, 8, 256], P('gx', 'gy'), may hold values from 0 to 2047
- latents: float32 [8, 8, 256, 512], P('gx', 'gy'), may hold values from -6 to 6
- gen_weight: float32 [8, 8, 512, 512], P('gx', 'gy'), may hold values from -6 to 6
- disc_weight: float32 [8, 8, 512, 512], P('gx', 'gy'), may hold values from -6 to 6
- disc_head: float32 [8, 8, 512], P('gx', 'gy'), may hold values from -6 to 6
Outputs:
- new_gen: float32 [8, 8, 512, 512], P('gx', 'gy')
- new_disc: float32 [8, 8, 512, 512], P('gx', 'gy')
- new_head: float32 [8, 8, 512], P('gx', 'gy')
All inputs are finite; a program needn't handle non-finite values.
Results may differ from a plain program's by a relative error of at most 0.0001.
Values sent between devices are 32-bit elements; how exact they have to be, the bound alone decides.
A program may use at most 128 MiB of HBM per device.

v0:
```python
import functools

import jax
import jax.numpy as jnp
from jax import lax
from jax.experimental import pallas as pl
from jax.experimental.pallas import tpu as pltpu
from jax.sharding import PartitionSpec as P

F32 = jnp.float32
NN = ((1,), (0,))
NT = ((1,), (1,))
TN = ((0,), (0,))


def split(x):
    high = x.astype(jnp.bfloat16)
    return high, (x - high.astype(F32)).astype(jnp.bfloat16)


def dot3(a, b, dims):
    d = lambda x, y: lax.dot_general(x, y, (dims, ((), ())), preferred_element_type=F32)
    return d(a[0], b[0]) + (d(a[0], b[1]) + d(a[1], b[0]))


def descend(value, grad):
    mean_sq = jnp.sum(jnp.sum(grad * grad, 0, keepdims=True), 1, keepdims=True) * (1.0 / grad.size)
    return value - 0.25 * grad * lax.rsqrt(mean_sq + 1e-06)


def kernel(
    nx, ny, gxn, gyn,
    samples, idx, lat, gen, disc, head,
    new_gen, new_disc, new_head,
    table, real, disc_h, head_h, lat_h, made_in, made_out, fake, back, gw, gh, whi, wlo,
    table_sem, disc_s, disc_r, head_s, head_r, lat_s, lat_r, made_s, made_r,
):
    cells, rows, width = lat.shape
    slots = 2 * nx + 2 * ny
    scale = width ** (-0.5)
    gx, gy = lax.axis_index("gx"), lax.axis_index("gy")
    above, below = lax.rem(gx + gxn - 1, gxn), lax.rem(gx + 1, gxn)
    before, after = lax.rem(gy + gyn - 1, gyn), lax.rem(gy + 1, gyn)

    table_copy = pltpu.make_async_copy(samples, table, table_sem)
    table_copy.start()

    barrier = pltpu.get_barrier_semaphore()
    for there in ({"gx": above}, {"gx": below}, {"gy": before}, {"gy": after}):
        pl.semaphore_signal(barrier, inc=1, device_id=there, device_id_type=pl.DeviceIdType.MESH)
    pl.semaphore_wait(barrier, 4)

    def remote(src, dst, send, recv, there):
        return pltpu.make_async_remote_copy(
            src_ref=src, dst_ref=dst, send_sem=send, recv_sem=recv,
            device_id=there, device_id_type=pl.DeviceIdType.MESH,
        )

    outgoing = []
    for i in range(nx):
        outgoing.append((2 * ny + i, i * ny + ny - 1, {"gy": after}))
        outgoing.append((2 * ny + nx + i, i * ny, {"gy": before}))
    for j in range(ny):
        outgoing.append((j, (nx - 1) * ny + j, {"gx": below}))
        outgoing.append((ny + j, j, {"gx": above}))

    head_out = [remote(head.at[c], head_h.at[s], head_s.at[s], head_r.at[s], t) for s, c, t in outgoing]
    disc_out = [remote(disc.at[c], disc_h.at[s], disc_s.at[s], disc_r.at[s], t) for s, c, t in outgoing]
    lat_out = [remote(lat.at[c], lat_h.at[s], lat_s.at[s], lat_r.at[s], t) for s, c, t in outgoing]
    for h, d in zip(head_out, disc_out):
        h.start()
        d.start()

    def arrived(buf, sem, s):
        remote(buf.at[s], buf.at[s], sem.at[s], sem.at[s], {"gx": above}).wait_recv()

    def row_slot(t):
        d, i = lax.rem(t // nx + gy + 1, 2), lax.rem(t, nx)
        return d, 2 * ny + d * nx + i, 2 * ny + (1 - d) * nx + i, i * ny + d * (ny - 1)

    def col_slot(t):
        d, j = t // ny, lax.rem(t, ny)
        return d, d * ny + j, (1 - d) * ny + j, d * (nx - 1) * ny + j

    pair_loops = []
    if nx > 1:
        half = (nx - 1) * ny
        def vertical(t, half=half):
            b, d = lax.rem(t, half), t // half
            return b + d * ny, b + (1 - d) * ny
        pair_loops.append((2 * half, vertical))
    if ny > 1:
        wide = nx * (ny - 1)
        def horizontal(t, wide=wide):
            b, d = lax.rem(t, wide), t // wide
            at = (b // (ny - 1)) * ny + lax.rem(b, ny - 1)
            return at + d, at + 1 - d
        pair_loops.append((2 * wide, horizontal))

    def slope_inner(hidden, top, real_side):
        score = scale * jnp.sum(hidden * top, 1, keepdims=True)
        slope = -jax.nn.sigmoid(-score) if real_side else 0.2 * jax.nn.sigmoid(score)
        return slope, (1.0 - hidden * hidden) * ((scale * slope) * top)

    def opponent(x, w, top):
        hidden = jnp.tanh(scale * dot3(split(x), w, NN))
        _, inner = slope_inner(hidden, top, True)
        return scale * dot3(split(inner), w, NT)

    def critic(x, c, real_side):
        xs = split(x)
        top = head[c]
        hidden = jnp.tanh(scale * dot3(xs, (whi[c], wlo[c]), NN))
        slope, inner = slope_inner(hidden, top, real_side)
        return scale * dot3(xs, split(inner), TN), scale * jnp.sum(slope * hidden, 0, keepdims=True)

    def add_critic(x, c):
        term_w, term_h = critic(x, c, False)
        gw[c] += term_w
        gh[c] += term_h

    def make(source, g):
        return jnp.tanh(scale * dot3(split(source), split(new_gen[g]), NN))

    def own(c, _):
        whi[c], wlo[c] = split(disc[c])
        fake[c] = jnp.tanh(scale * dot3(split(lat[c]), split(gen[c]), NN))
        back[c] = opponent(fake[c], (whi[c], wlo[c]), head[c])
        return 0

    lax.fori_loop(0, cells, own, 0)
    for count, pair in pair_loops:
        def local_opponent(t, _, pair=pair):
            c, n = pair(t)
            back[c] += opponent(fake[c], (whi[n], wlo[n]), head[n])
            return 0
        lax.fori_loop(0, count, local_opponent, 0)

    table_copy.wait()

    def real_term(c, _):
        def fetch(b, _):
            for k in range(8):
                r = b * 8 + k
                real[pl.ds(r, 1), :] = table[pl.ds(idx[c, r], 1), :]
            return 0
        lax.fori_loop(0, rows // 8, fetch, 0)
        gw[c], gh[c] = critic(real[...], c, True)
        return 0

    lax.fori_loop(0, cells, real_term, 0)

    def far_opponent(where):
        def body(t, _):
            _, s, _, c = where(t)
            arrived(head_h, head_r, s)
            arrived(disc_h, disc_r, s)
            back[c] += opponent(fake[c], split(disc_h[s]), head_h[s])
            return 0
        return body

    for h, d, l in zip(head_out, disc_out, lat_out):
        h.wait_send()
        d.wait_send()
        l.start()
    lax.fori_loop(0, 2 * nx, far_opponent(row_slot), 0)
    lax.fori_loop(0, 2 * ny, far_opponent(col_slot), 0)

    def update(c, _):
        f = fake[c]
        grad = scale * dot3(split(lat[c]), split((1.0 - f * f) * back[c]), TN)
        new_gen[c] = descend(gen[c], grad)
        return 0

    lax.fori_loop(0, cells, update, 0)

    def made_copy(where, axis, t):
        d, s, there, _ = where(t)
        me, n = (gx, gxn) if axis == "gx" else (gy, gyn)
        target = lax.rem(me + n + 2 * d - 1, n)
        return remote(made_out.at[s], made_in.at[there], made_s.at[s], made_r.at[there], {axis: target})

    def far_make(where, axis):
        def body(t, _):
            _, s, _, c = where(t)
            arrived(lat_h, lat_r, s)
            made_out[s] = make(lat_h[s], c)
            made_copy(where, axis, t).start()
            return 0
        return body

    lax.fori_loop(0, 2 * nx, far_make(row_slot, "gy"), 0)
    lax.fori_loop(0, 2 * ny, far_make(col_slot, "gx"), 0)

    def own_critic(c, _):
        add_critic(make(lat[c], c), c)
        return 0

    lax.fori_loop(0, cells, own_critic, 0)
    for count, pair in pair_loops:
        def local_critic(t, _, pair=pair):
            c, n = pair(t)
            add_critic(make(lat[c], n), c)
            return 0
        lax.fori_loop(0, count, local_critic, 0)

    def far_critic(where):
        def body(t, _):
            _, s, _, c = where(t)
            arrived(made_in, made_r, s)
            add_critic(made_in[s], c)
            return 0
        return body

    lax.fori_loop(0, 2 * nx, far_critic(row_slot), 0)
    lax.fori_loop(0, 2 * ny, far_critic(col_slot), 0)

    def finish(c, _):
        new_disc[c] = descend(disc[c], gw[c])
        new_head[c] = descend(head[c], gh[c])
        return 0

    lax.fori_loop(0, cells, finish, 0)
    for l in lat_out:
        l.wait_send()
    for t in range(2 * nx):
        made_copy(row_slot, "gy", t).wait_send()
    for t in range(2 * ny):
        made_copy(col_slot, "gx", t).wait_send()


def local(gxn, gyn, samples, real_idx, latents, gen_weight, disc_weight, disc_head):
    nx, ny, rows, width = latents.shape
    cells, slots = nx * ny, 2 * (nx + ny)
    vmem = pl.BlockSpec(memory_space=pltpu.VMEM)
    square, block, line = (width, width), (rows, width), (1, width)
    dma = lambda: pltpu.SemaphoreType.DMA((slots,))
    outs = pl.pallas_call(
        functools.partial(kernel, nx, ny, gxn, gyn),
        out_shape=(
            jax.ShapeDtypeStruct((cells,) + square, F32),
            jax.ShapeDtypeStruct((cells,) + square, F32),
            jax.ShapeDtypeStruct((cells,) + line, F32),
        ),
        in_specs=[pl.BlockSpec(memory_space=pl.ANY), pl.BlockSpec(memory_space=pltpu.SMEM)] + [vmem] * 4,
        out_specs=(vmem, vmem, vmem),
        scratch_shapes=[
            pltpu.VMEM(samples.shape, F32),
            pltpu.VMEM(block, F32),
            pltpu.VMEM((slots,) + square, F32),
            pltpu.VMEM((slots,) + line, F32),
            pltpu.VMEM((slots,) + block, F32),
            pltpu.VMEM((slots,) + block, F32),
            pltpu.VMEM((slots,) + block, F32),
            pltpu.VMEM((cells,) + block, F32),
            pltpu.VMEM((cells,) + block, F32),
            pltpu.VMEM((cells,) + square, F32),
            pltpu.VMEM((cells,) + line, F32),
            pltpu.VMEM((cells,) + square, jnp.bfloat16),
            pltpu.VMEM((cells,) + square, jnp.bfloat16),
            pltpu.SemaphoreType.DMA,
        ] + [dma() for _ in range(8)],
        compiler_params=pltpu.CompilerParams(
            collective_id=0, has_side_effects=True, vmem_limit_bytes=58 * 1024 * 1024
        ),
        name="coev",
    )(
        samples,
        real_idx.reshape(cells, rows),
        latents.reshape((cells,) + block),
        gen_weight.reshape((cells,) + square),
        disc_weight.reshape((cells,) + square),
        disc_head.reshape((cells,) + line),
    )
    return outs[0].reshape(gen_weight.shape), outs[1].reshape(disc_weight.shape), outs[2].reshape(disc_head.shape)


def solution(mesh):
    cells3, cells4 = P("gx", "gy", None), P("gx", "gy", None, None)
    return jax.shard_map(
        functools.partial(local, mesh.shape["gx"], mesh.shape["gy"]),
        mesh=mesh,
        in_specs=(P(), cells3, cells4, cells4, cells4, cells3),
        out_specs=(cells4, cells4, cells3),
        check_vma=False,
    )
```

profile of v0, /device:TPU:0, one launch (start us, length us, event | category | flops | bytes accessed | tf_op | source)
XLA Modules:
  0.0 114.5 jit_solution(16306977312633884965)
XLA Ops:
  0.6 1.3 %copy.13 = s32[2,1,256]{2,0,1:T(2,128)} copy(s32[2,1,256]{2,1,0:T(1,128)} %param.7) | data formatting | bytes 4096
  1.9 107.5 %coev.1 = (f32[2,512,512]{2,1,0:T(8,128)}, f32[2,512,512]{2,1,0:T(8,128)}, f32[2,1,512]{2,1,0:T(1,128)}) custom-call(f32[2048,512]{1,0:T(8,128)} %samples.1, s32[2,256]{1,0:T(2,128)} %bitcast.17, f32[2,256,512]{2,1,0:T(8,128)} %bitcast.16, f32[2,512,512]{2,1,0:T(8,128)} %bitcast.12, f32[2,512,512]{2,1,0:T(8,128)} %bitcast.13, f32[2,1,512]{2,1,0:T(1,128)} %head.1), custom_call_target="tpu_custom_call" | custom-call | tf_op jit(solution)/shard_map/coev/pallas_call | solution.py:238
  109.4 0.0 copy-start
  109.4 3.2 %copy.17 = f32[2,1,512,512]{3,2,1,0:T(8,128)} copy(f32[2,1,512,512]{3,2,1,0:T(8,128)} %bitcast.15) | data formatting | bytes 4194304
  112.6 0.0 copy-done
  112.6 0.0 copy-start.1
  112.6 1.3 %copy.18 = f32[2,1,512,512]{3,2,1,0:T(8,128)} copy(f32[2,1,512,512]{3,2,1,0:T(8,128)S(1)} %bitcast.14) | data formatting | bytes 4194304
  113.9 0.0 copy-done.1
  113.9 0.6 copy.19
Async XLA Ops:
  109.4 3.2 %copy-start = (f32[2,512,512]{2,1,0:T(8,128)S(1)}, f32[2,512,512]{2,1,0:T(8,128)}, u32[]{:S(2)}) copy-start(f32[2,512,512]{2,1,0:T(8,128)} %get-tuple-element.7) | copy-start | bytes 6291460
  112.6 1.3 %copy-start.1 = (f32[2,1,512]{2,1,0:T(1,128)S(1)}, f32[2,1,512]{2,1,0:T(1,128)}, u32[]{:S(2)}) copy-start(f32[2,1,512]{2,1,0:T(1,128)} %get-tuple-element.17) | copy-start | bytes 12292
where the time goes:
time: 115 us
  Pallas kernels  107 us (93%)
  local copies, waits for them, and re-layouts  6.41 us (6%)
    pallas_call x1, Pallas kernels, local(): pl.pallas_call(functools.partial(kernel, nx, ny, gxn, gyn), out_shape=(ja...  107 us
    unnamed x8, local copies, waits for them, and re-layouts  6.41 us

commit v1 on v0

--- a/solution.py
+++ b/solution.py
@@ -30,10 +30,10 @@
 
 def kernel(
     nx, ny, gxn, gyn,
-    samples, idx, lat, gen, disc, head,
-    new_gen, new_disc, new_head,
-    table, real, disc_h, head_h, lat_h, made_in, made_out, fake, back, gw, gh, whi, wlo,
-    table_sem, disc_s, disc_r, head_s, head_r, lat_s, lat_r, made_s, made_r,
+    samples, idx, lat_in, gen_in, disc_in, head,
+    gen_out, disc_out_ref, new_head,
+    lat, gen, disc, new_gen, new_disc, table, real, disc_h, head_h, lat_h, made_in, made_out, fake, back, gw, gh, whi, wlo,
+    table_sem, in_sems, out_sems, disc_s, disc_r, head_s, head_r, lat_s, lat_r, made_s, made_r,
 ):
     cells, rows, width = lat.shape
     slots = 2 * nx + 2 * ny
@@ -42,12 +42,15 @@
     above, below = lax.rem(gx + gxn - 1, gxn), lax.rem(gx + 1, gxn)
     before, after = lax.rem(gy + gyn - 1, gyn), lax.rem(gy + 1, gyn)
 
-    table_copy = pltpu.make_async_copy(samples, table, table_sem)
-    table_copy.start()
-
     barrier = pltpu.get_barrier_semaphore()
     for there in ({"gx": above}, {"gx": below}, {"gy": before}, {"gy": after}):
         pl.semaphore_signal(barrier, inc=1, device_id=there, device_id_type=pl.DeviceIdType.MESH)
+    loads = [
+        pltpu.make_async_copy(src, dst, in_sems.at[k])
+        for k, (src, dst) in enumerate(((disc_in, disc), (lat_in, lat), (gen_in, gen)))
+    ]
+    for load in loads:
+        load.start()
     pl.semaphore_wait(barrier, 4)
 
     def remote(src, dst, send, recv, there):
@@ -65,11 +68,15 @@
         outgoing.append((ny + j, j, {"gx": above}))
 
     head_out = [remote(head.at[c], head_h.at[s], head_s.at[s], head_r.at[s], t) for s, c, t in outgoing]
-    disc_out = [remote(disc.at[c], disc_h.at[s], disc_s.at[s], disc_r.at[s], t) for s, c, t in outgoing]
-    lat_out = [remote(lat.at[c], lat_h.at[s], lat_s.at[s], lat_r.at[s], t) for s, c, t in outgoing]
+    disc_out = [remote(disc_in.at[c], disc_h.at[s], disc_s.at[s], disc_r.at[s], t) for s, c, t in outgoing]
+    lat_out = [remote(lat_in.at[c], lat_h.at[s], lat_s.at[s], lat_r.at[s], t) for s, c, t in outgoing]
     for h, d in zip(head_out, disc_out):
+        d.start()
         h.start()
-        d.start()
+    table_copy = pltpu.make_async_copy(samples, table, table_sem)
+    table_copy.start()
+    for load in loads:
+        load.wait()
 
     def arrived(buf, sem, s):
         remote(buf.at[s], buf.at[s], sem.at[s], sem.at[s], {"gx": above}).wait_recv()
@@ -142,7 +149,7 @@
         def fetch(b, _):
             for k in range(8):
                 r = b * 8 + k
-                real[pl.ds(r, 1), :] = table[pl.ds(idx[c, r], 1), :]
+                real[pl.ds(r, 1), :] = table[pl.ds(idx[c // ny, lax.rem(c, ny), r], 1), :]
             return 0
         lax.fori_loop(0, rows // 8, fetch, 0)
         gw[c], gh[c] = critic(real[...], c, True)
@@ -159,17 +166,22 @@
             return 0
         return body
 
+    lax.fori_loop(0, nx, far_opponent(row_slot), 0)
     for h, d, l in zip(head_out, disc_out, lat_out):
         h.wait_send()
         d.wait_send()
         l.start()
-    lax.fori_loop(0, 2 * nx, far_opponent(row_slot), 0)
+    lax.fori_loop(nx, 2 * nx, far_opponent(row_slot), 0)
     lax.fori_loop(0, 2 * ny, far_opponent(col_slot), 0)
+
+    def store(src, dst, k, c):
+        return pltpu.make_async_copy(src.at[c], dst.at[c], out_sems.at[k, c])
 
     def update(c, _):
         f = fake[c]
         grad = scale * dot3(split(lat[c]), split((1.0 - f * f) * back[c]), TN)
         new_gen[c] = descend(gen[c], grad)
+        store(new_gen, gen_out, 0, c).start()
         return 0
 
     lax.fori_loop(0, cells, update, 0)
@@ -217,6 +229,7 @@
 
     def finish(c, _):
         new_disc[c] = descend(disc[c], gw[c])
+        store(new_disc, disc_out_ref, 1, c).start()
         new_head[c] = descend(head[c], gh[c])
         return 0
 
@@ -227,12 +240,15 @@
         made_copy(row_slot, "gy", t).wait_send()
     for t in range(2 * ny):
         made_copy(col_slot, "gx", t).wait_send()
+    for c in range(cells):
+        store(new_gen, gen_out, 0, c).wait()
+        store(new_disc, disc_out_ref, 1, c).wait()
 
 
 def local(gxn, gyn, samples, real_idx, latents, gen_weight, disc_weight, disc_head):
     nx, ny, rows, width = latents.shape
     cells, slots = nx * ny, 2 * (nx + ny)
-    vmem = pl.BlockSpec(memory_space=pltpu.VMEM)
+    vmem, hbm = pl.BlockSpec(memory_space=pltpu.VMEM), pl.BlockSpec(memory_space=pl.ANY)
     square, block, line = (width, width), (rows, width), (1, width)
     dma = lambda: pltpu.SemaphoreType.DMA((slots,))
     outs = pl.pallas_call(
@@ -242,9 +258,14 @@
             jax.ShapeDtypeStruct((cells,) + square, F32),
             jax.ShapeDtypeStruct((cells,) + line, F32),
         ),
-        in_specs=[pl.BlockSpec(memory_space=pl.ANY), pl.BlockSpec(memory_space=pltpu.SMEM)] + [vmem] * 4,
-        out_specs=(vmem, vmem, vmem),
+        in_specs=[hbm, pl.BlockSpec(memory_space=pltpu.SMEM), hbm, hbm, hbm, vmem],
+        out_specs=(hbm, hbm, vmem),
         scratch_shapes=[
+            pltpu.VMEM((cells,) + block, F32),
+            pltpu.VMEM((cells,) + square, F32),
+            pltpu.VMEM((cells,) + square, F32),
+            pltpu.VMEM((cells,) + square, F32),
+            pltpu.VMEM((cells,) + square, F32),
             pltpu.VMEM(samples.shape, F32),
             pltpu.VMEM(block, F32),
             pltpu.VMEM((slots,) + square, F32),
@@ -259,6 +280,8 @@
             pltpu.VMEM((cells,) + square, jnp.bfloat16),
             pltpu.VMEM((cells,) + square, jnp.bfloat16),
             pltpu.SemaphoreType.DMA,
+            pltpu.SemaphoreType.DMA((3,)),
+            pltpu.SemaphoreType.DMA((2, cells)),
         ] + [dma() for _ in range(8)],
         compiler_params=pltpu.CompilerParams(
             collective_id=0, has_side_effects=True, vmem_limit_bytes=58 * 1024 * 1024
@@ -266,7 +289,7 @@
         name="coev",
     )(
         samples,
-        real_idx.reshape(cells, rows),
+        real_idx,
         latents.reshape((cells,) + block),
         gen_weight.reshape((cells,) + square),
         disc_weight.reshape((cells,) + square),

time: 115 us -> 111 us (0.965)
  Pallas kernels: 107 us -> 105 us
  local copies, waits for them, and re-layouts: 6.41 us -> 5.15 us
    pallas_call x1, Pallas kernels: 107 us -> 105 us  [local(): pl.pallas_call(functools.partial(kernel, nx, ny, gxn, gyn), out_shape=(ja...]
    unnamed x8 -> x7, local copies, waits for them, and re-layouts: 6.41 us -> 5.15 us
where the time goes in v1:
time: 111 us
  Pallas kernels  105 us (95%)
  local copies, waits for them, and re-layouts  5.15 us (5%)
    pallas_call x1, Pallas kernels, local(): pl.pallas_call(functools.partial(kernel, nx, ny, gxn, gyn), out_shape=(ja...  105 us
    unnamed x7, local copies, waits for them, and re-layouts  5.15 us

profile of v1, /device:TPU:0, one launch (start us, length us, event | category | flops | bytes accessed | tf_op | source)
XLA Modules:
  0.0 111.3 jit_solution(5249807054810742460)
XLA Ops:
  0.6 105.5 %coev.1 = (f32[2,512,512]{2,1,0:T(8,128)}, f32[2,512,512]{2,1,0:T(8,128)}, f32[2,1,512]{2,1,0:T(1,128)}) custom-call(f32[2048,512]{1,0:T(8,128)} %samples.1, s32[2,1,256]{2,1,0:T(1,128)} %idx.1, f32[2,256,512]{2,1,0:T(8,128)} %bitcast.13, f32[2,512,512]{2,1,0:T(8,128)} %bitcast.9, f32[2,512,512]{2,1,0:T(8,128)} %bitcast.10, f32[2,1,512]{2,1,0:T(1,128)} %head.1), custom_call_target="tpu_custom_call" | custom-call | tf_op jit(solution)/shard_map/coev/pallas_call | solution.py:254
  106.1 0.0 copy-start
  106.1 3.2 %copy.14 = f32[2,1,512,512]{3,2,1,0:T(8,128)} copy(f32[2,1,512,512]{3,2,1,0:T(8,128)} %bitcast.12) | data formatting | bytes 4194304
  109.3 0.0 copy-done
  109.3 0.0 copy-start.1
  109.3 1.3 %copy.15 = f32[2,1,512,512]{3,2,1,0:T(8,128)} copy(f32[2,1,512,512]{3,2,1,0:T(8,128)S(1)} %bitcast.11) | data formatting | bytes 4194304
  110.7 0.0 copy-done.1
  110.7 0.6 copy.16
Async XLA Ops:
  106.1 3.2 %copy-start = (f32[2,512,512]{2,1,0:T(8,128)S(1)}, f32[2,512,512]{2,1,0:T(8,128)}, u32[]{:S(2)}) copy-start(f32[2,512,512]{2,1,0:T(8,128)} %get-tuple-element.7) | copy-start | bytes 6291460
  109.3 1.3 %copy-start.1 = (f32[2,1,512]{2,1,0:T(1,128)S(1)}, f32[2,1,512]{2,1,0:T(1,128)}, u32[]{:S(2)}) copy-start(f32[2,1,512]{2,1,0:T(1,128)} %get-tuple-element.17) | copy-start | bytes 12292

commit v2 on v1

--- a/solution.py
+++ b/solution.py
@@ -192,17 +192,21 @@
         target = lax.rem(me + n + 2 * d - 1, n)
         return remote(made_out.at[s], made_in.at[there], made_s.at[s], made_r.at[there], {axis: target})
 
-    def far_make(where, axis):
+    def far_make(where, axis, send):
         def body(t, _):
             _, s, _, c = where(t)
             arrived(lat_h, lat_r, s)
             made_out[s] = make(lat_h[s], c)
-            made_copy(where, axis, t).start()
+            if send:
+                made_copy(where, axis, t).start()
             return 0
         return body
 
-    lax.fori_loop(0, 2 * nx, far_make(row_slot, "gy"), 0)
-    lax.fori_loop(0, 2 * ny, far_make(col_slot, "gx"), 0)
+    mid = nx + (nx + 1) // 2
+    lax.fori_loop(0, mid, far_make(row_slot, "gy", True), 0)
+    lax.fori_loop(0, ny, far_make(col_slot, "gx", True), 0)
+    lax.fori_loop(mid, 2 * nx, far_make(row_slot, "gy", False), 0)
+    lax.fori_loop(ny, 2 * ny, far_make(col_slot, "gx", False), 0)
 
     def own_critic(c, _):
         add_critic(make(lat[c], c), c)
@@ -216,6 +220,15 @@
             return 0
         lax.fori_loop(0, count, local_critic, 0)
 
+    for t in range(mid):
+        made_copy(row_slot, "gy", t).wait_send()
+    for t in range(mid, 2 * nx):
+        made_copy(row_slot, "gy", t).start()
+    for t in range(ny):
+        made_copy(col_slot, "gx", t).wait_send()
+    for t in range(ny, 2 * ny):
+        made_copy(col_slot, "gx", t).start()
+
     def far_critic(where):
         def body(t, _):
             _, s, _, c = where(t)
@@ -224,8 +237,13 @@
             return 0
         return body
 
-    lax.fori_loop(0, 2 * nx, far_critic(row_slot), 0)
-    lax.fori_loop(0, 2 * ny, far_critic(col_slot), 0)
+    def far_row(t, _):
+        return far_critic(row_slot)(t, 0)
+
+    lax.fori_loop(0, mid, far_row, 0)
+    lax.fori_loop(0, ny, lambda t, _: far_critic(col_slot)(lax.rem(t + ny, 2 * ny), 0), 0)
+    lax.fori_loop(mid, 2 * nx, far_row, 0)
+    lax.fori_loop(ny, 2 * ny, lambda t, _: far_critic(col_slot)(t - ny, 0), 0)
 
     def finish(c, _):
         new_disc[c] = descend(disc[c], gw[c])
@@ -236,13 +254,28 @@
     lax.fori_loop(0, cells, finish, 0)
     for l in lat_out:
         l.wait_send()
-    for t in range(2 * nx):
+    for t in range(mid, 2 * nx):
         made_copy(row_slot, "gy", t).wait_send()
-    for t in range(2 * ny):
+    for t in range(ny, 2 * ny):
         made_copy(col_slot, "gx", t).wait_send()
     for c in range(cells):
         store(new_gen, gen_out, 0, c).wait()
         store(new_disc, disc_out_ref, 1, c).wait()
+
+
+def hand_over(gen_in, disc_in, head_in, gen_out, disc_out, head_out, sems):
+    copies = [pltpu.make_async_copy(head_in, head_out, sems.at[2, 0, 0])]
+    cells, width, _ = gen_in.shape
+    half = width // 2
+    for k, (src, dst) in enumerate(((gen_in, gen_out), (disc_in, disc_out))):
+        for c in range(cells):
+            for p in range(2):
+                part = pl.ds(p * half, half)
+                copies.append(pltpu.make_async_copy(src.at[c, part], dst.at[c, part], sems.at[k, c, p]))
+    for copy in copies:
+        copy.start()
+    for copy in copies:
+        copy.wait()
 
 
 def local(gxn, gyn, samples, real_idx, latents, gen_weight, disc_weight, disc_head):
@@ -295,6 +328,14 @@
         disc_weight.reshape((cells,) + square),
         disc_head.reshape((cells,) + line),
     )
+    outs = pl.pallas_call(
+        hand_over,
+        out_shape=tuple(jax.ShapeDtypeStruct(o.shape, F32) for o in outs),
+        in_specs=[hbm] * 3,
+        out_specs=(hbm,) * 3,
+        scratch_shapes=[pltpu.SemaphoreType.DMA((3, cells, 2))],
+        name="hand_over",
+    )(*outs)
     return outs[0].reshape(gen_weight.shape), outs[1].reshape(disc_weight.shape), outs[2].reshape(disc_head.shape)
 
 

time: 111 us -> 233 us (2.10)
  Pallas kernels: 105 us -> 231 us
  local copies, waits for them, and re-layouts: 5.15 us -> 0 us
    pallas_call x0 -> x1, Pallas kernels: none -> 128 us  [local(): pl.pallas_call(hand_over, out_shape=tuple((jax.ShapeDtypeStruct(o.shape,...]
    unnamed x7 -> x0, local copies, waits for them, and re-layouts: 5.15 us -> none
    pallas_call x1, Pallas kernels: 105 us -> 103 us  [local(): pl.pallas_call(functools.partial(kernel, nx, ny, gxn, gyn), out_shape=(ja...]
where the time goes in v2:
time: 233 us; the launch traced here: 232 us
  Pallas kernels  231 us (99%)
    pallas_call x1, Pallas kernels, local(): pl.pallas_call(hand_over, out_shape=tuple((jax.ShapeDtypeStruct(o.shape,...  128 us
    pallas_call x1, Pallas kernels, local(): pl.pallas_call(functools.partial(kernel, nx, ny, gxn, gyn), out_shape=(ja...  103 us

profile of v2, /device:TPU:0, one launch (start us, length us, event | category | flops | bytes accessed | tf_op | source)
XLA Modules:
  0.0 232.1 jit_solution(9470581968164302207)
XLA Ops:
  0.6 102.9 %coev.1 = (f32[2,512,512]{2,1,0:T(8,128)}, f32[2,512,512]{2,1,0:T(8,128)}, f32[2,1,512]{2,1,0:T(1,128)}) custom-call(f32[2048,512]{1,0:T(8,128)} %samples.1, s32[2,1,256]{2,1,0:T(1,128)} %idx.1, f32[2,256,512]{2,1,0:T(8,128)} %bitcast.11, f32[2,512,512]{2,1,0:T(8,128)} %bitcast.9, f32[2,512,512]{2,1,0:T(8,128)} %bitcast.10, f32[2,1,512]{2,1,0:T(1,128)} %head.1), custom_call_target="tpu_custom_call" | custom-call | tf_op jit(solution)/shard_map/coev/pallas_call | solution.py:287
  103.5 128.4 %hand_over.1 = (f32[2,512,512]{2,1,0:T(8,128)}, f32[2,512,512]{2,1,0:T(8,128)}, f32[2,1,512]{2,1,0:T(1,128)}) custom-call(f32[2,512,512]{2,1,0:T(8,128)} %get-tuple-element.9.gen_in, f32[2,512,512]{2,1,0:T(8,128)} %get-tuple-element.10.disc_in, f32[2,1,512]{2,1,0:T(1,128)} %get-tuple-element.11.head_in), custom_call_target="tpu_custom_call" | custom-call | tf_op jit(solution)/shard_map/hand_over/pallas_call | solution.py:331
